TPU v7x, 128 devices: a whole 4x4x4 slice. The times are simulated.
128 devices in a mesh: row: 16 (over y, x), col: 8 (over z, core).
Axes of the slice: x: 4, y: 4, z: 4, core: 2. Of those that a mesh axis runs over, the one named last changes fastest.
Arguments:
- band_tiles: bfloat16 [16, 128, 256, 256], P('row', 'col'), may hold values from 0.0009994507 to 1
- band_cell: int32 [16, 128], P('row', 'col'), may hold values from 0 to 31, as said below
- band_count: int32 [16, 8], P('row', 'col'), may hold values from 1 to 16, as said below
- matrix_tiles: bfloat16 [16, 64, 256, 256], P('row', 'col'), may hold values from 7.390976e-05 to 0.07421875
- matrix_col: int32 [16, 64], P('row', 'col'), may hold values from 0 to 15
- matrix_live: int32 [16, 64], P('row', 'col'), may hold values 0 or 1
Outputs:
- reached: bfloat16 [8192, 32768], P('row', 'col')
- gained: float32 [], replicated
Inputs may be any that keep to these rules, and one draw needn't show every extreme that they name: The band_cell values of one device's 16 slots are distinct. `band_count`: among the 8 devices of one index of row, the live slots with slot number 16 // 2 or more number at most 8 in all.
All inputs are finite; a program needn't handle non-finite values. No bound on the sum of `matrix_live` on one device may be relied on, other than what follows from the above.
Results may differ from a plain program's by a relative error of at most 0.001.
Values may be sent and summed in bfloat16 or wider, within the bound.
A program may use at most 128 MiB of HBM per device.

v0:
```python
import jax
import jax.numpy as jnp
from jax import lax
from jax.sharding import Mesh
from jax.sharding import PartitionSpec as P

TILES = 128
BR = 2
COL = ("col_0", "col_1")
ROW = ("row_0", "row_1")
ROW_COL = ("row_0", "row_1", "col_0", "col_1")


def rows_for(lines, length):
    spare = -lines.shape[0] % length
    if not spare:
        return lines
    return jnp.concatenate([lines, jnp.zeros((spare, *lines.shape[1:]), lines.dtype)])


def sum_by_parts(shard, axis):
    lines = shard.reshape(-1, *shard.shape[1:][-1:])
    own = lax.psum_scatter(
        rows_for(lines, lax.axis_size(axis)), axis, scatter_dimension=0, tiled=True
    )
    whole = lax.all_gather(own, axis).reshape(-1, *lines.shape[1:])
    return lax.slice_in_dim(whole, 0, len(lines)).reshape(shard.shape)


def over_axes(shard, axes):
    for axis in axes:
        shard = lax.psum(shard, axis)
    return shard


def on_device(band_tiles, band_cell, band_count, matrix_tiles, matrix_col, matrix_live):
    slots_own = band_tiles.shape[1]
    tile = band_tiles.shape[-1]
    n_col = lax.axis_size(COL)
    tcols = TILES // n_col
    places = BR * tcols
    spots = jnp.arange(places, dtype=jnp.int32)
    b_tiles, b_index, b_live = (
        lax.all_gather(matrix_tiles, ROW, axis=0, tiled=True),
        lax.all_gather(matrix_col, ROW, axis=0, tiled=True),
        lax.all_gather(matrix_live, ROW, axis=0, tiled=True),
    )
    flat_tiles = b_tiles.reshape(-1, tile, tile)
    half = slots_own // 2
    front_tiles, a_cell, a_count = (
        lax.all_gather(band_tiles[:, :half], COL, axis=1, tiled=True),
        lax.all_gather(band_cell, COL, axis=1, tiled=True),
        lax.all_gather(band_count, COL, axis=1, tiled=True),
    )
    counts = a_count[0]
    spill = jnp.maximum(counts - half, 0)
    before = jnp.cumsum(spill) - spill
    ending = before + spill
    mine = lax.axis_index(COL)
    own_before = jnp.take(before, mine)
    own_spill = jnp.maximum(band_count[0, 0] - half, 0)
    pack_spot = jnp.arange(half, dtype=jnp.int32)
    upper = jnp.arange(half, dtype=jnp.int32)
    place_w = (
        (pack_spot[:, None] == own_before + upper[None, :]) & (upper[None, :] < own_spill)
    ).astype(jnp.bfloat16)
    packed = jnp.einsum(
        "qs,sxy->qxy", place_w, band_tiles[0, half:], preferred_element_type=jnp.float32
    )
    spilled = (
        sum_by_parts(packed.astype(jnp.bfloat16), COL).astype(jnp.float32).astype(jnp.bfloat16)
    )
    holder = jnp.sum((ending[None, :] <= pack_spot[:, None]).astype(jnp.int32), axis=1)
    holder = jnp.clip(holder, 0, n_col - 1)
    spill_slot = jnp.clip(half + pack_spot - jnp.take(before, holder), 0, slots_own - 1)
    spill_cell = jnp.take(a_cell[0], holder * slots_own + spill_slot)
    spill_valid = pack_spot < jnp.sum(spill)
    front = jnp.arange(n_col * half, dtype=jnp.int32)
    front_source = front // half
    front_slot = front % half
    front_cell = jnp.take(a_cell[0], front_source * slots_own + front_slot)
    front_valid = front_slot < jnp.take(counts, front_source)
    sources = jnp.concatenate([front_source, holder])
    cells = jnp.concatenate([front_cell, spill_cell])
    valid = jnp.concatenate([front_valid, spill_valid])
    tiles = jnp.concatenate([front_tiles[0], spilled], axis=0)
    k_glob = sources * tcols + cells % tcols
    i_loc = cells // tcols
    picked = jnp.take(flat_tiles, k_glob, axis=0)
    picked_index = jnp.take(b_index.reshape(-1), k_glob)
    picked_live = jnp.take(b_live.reshape(-1), k_glob)
    live = (picked_live > 0) & valid
    position = i_loc * tcols + picked_index
    product = jnp.einsum("axy,ayz->axz", tiles, picked, preferred_element_type=jnp.float32)
    weights = ((position[:, None] == spots[None, :]) & live[:, None]).astype(jnp.float32)
    summed = jnp.einsum("ap,axz->pxz", weights, product, precision=lax.Precision.HIGHEST)
    own_live = jnp.arange(slots_own, dtype=jnp.int32) < band_count[0, 0]
    own_w = ((band_cell[0][:, None] == spots[None, :]) & own_live[:, None]).astype(jnp.bfloat16)
    base = jnp.einsum("sp,sxz->pxz", own_w, band_tiles[0], preferred_element_type=jnp.float32)
    expanded = jnp.minimum(1.0, base + summed)
    block = (
        expanded.reshape(BR, tcols, tile, tile)
        .transpose(0, 2, 1, 3)
        .reshape(BR * tile, tcols * tile)
    )
    total = over_axes(jnp.sum(expanded - base), ROW_COL)
    devices = lax.axis_size(ROW) * n_col
    gained = total / (tile * tile * devices * places)
    return (block.astype(jnp.bfloat16), gained)


def solution(mesh):
    split = Mesh(mesh.devices.reshape(4, 4, 4, 2), ("row_0", "row_1", "col_0", "col_1"))
    placed = (
        P(ROW, COL, None, None),
        P(ROW, COL),
        P(ROW, COL),
        P(ROW, COL, None, None),
        P(ROW, COL),
        P(ROW, COL),
    )
    return jax.shard_map(
        on_device, mesh=split, in_specs=placed, out_specs=(P(ROW, COL), P()), check_vma=False
    )
```

profile of v0, /device:TPU:1, one launch (start us, length us, event | category | flops | bytes accessed | tf_op | source)
XLA Modules:
  0.0 311.7 jit_solution(18201135137651149009)
XLA Ops:
  8.0 0.0 copy-start
  8.0 0.0 copy-start.2
  8.0 0.0 copy-start.3
  8.0 0.0 reduce-scatter.2.cloned.1.call-start
  8.9 1.2 dynamic-slice.3
  10.8 0.7 bitcast_dynamic-update-slice_fusion
  11.5 0.8 bitcast_dynamic-update-slice_fusion.1
  12.2 9.8 %all-reduce.2 = (s32[8]{0:T(128)S(1)}, s32[128]{0:T(128)S(1)}) all-reduce(s32[8]{0:T(128)S(1)} %bitcast_dynamic-update-slice_fusion, s32[128]{0:T(128)S(1)} %bitcast_dynamic-update-slice_fusion.1), channel_id=1, replica_groups=mesh['row_0'=4,'row_1'=4,'col_0'=4,'col_1'=2] {'col_0','col_1'}, use_global_device_ids=true, to_apply=%add.1 | all-reduce | flops 136 | bytes 1088
  22.0 0.6 fusion.42
  22.6 0.2 reduce-window.8
  22.8 0.6 dynamic-slice.2
  24.1 1.3 slice.7
  25.4 0.7 convolution_convert_fusion
  26.1 1.2 copy.24
  27.2 0.0 reduce-scatter.2.cloned.1.call-update
  27.3 0.0 all-gather.9.cloned.1.call-start
  27.3 0.5 all-gather.9.cloned.1.call-update
  27.8 0.0 all-gather.11.cloned.1.call-start
  27.9 29.4 %reduce-scatter.2.cloned.1.call-done = bf16[256,256]{1,0:T(8,128)(2,1)} async-done(((bf16[2048,256]{1,0:T(8,128)(2,1)}), bf16[256,256]{1,0:T(8,128)(2,1)}) %reduce-scatter.2.cloned.1.call-update) | async-done | bytes 131088 | tf_op jit(solution)/shard_map/reduce_scatter | solution.py:23
  57.3 0.0 all-gather.11.cloned.1.call-update
  57.3 0.0 all-gather.7.cloned.1.call-start
  57.4 0.0 copy-done
  57.4 1.0 slice.43
  58.4 0.0 all-gather.7.cloned.1.call-update
  58.4 0.1 convert_reduce_fusion
  58.6 0.6 gather_fusion.1
  59.3 0.6 gather_fusion.2
  59.9 0.8 gather_fusion
  60.7 0.0 copy-done.2
  60.7 17.2 %all-gather.1 = s32[16,1,8]{2,1,0:T(1,128)S(1)} all-gather(s32[1,1,8]{2,1,0:T(1,128)S(1)} %bitcast.102), channel_id=1, replica_groups=mesh['row_0'=4,'row_1'=4,'col_0'=4,'col_1'=2] {'row_0','row_1'}, dimensions={0}, use_global_device_ids=true | all-gather | bytes 544 | tf_op jit(solution)/shard_map/all_gather | solution.py:45
  77.9 0.5 broadcast.1065
  78.4 0.7 reduce.7
  79.1 0.1 reshape.382
  79.2 0.0 copy-done.3
  79.2 17.3 %all-gather.2 = s32[16,1,8]{2,1,0:T(1,128)S(1)} all-gather(s32[1,1,8]{2,1,0:T(1,128)S(1)} %bitcast.103), channel_id=1, replica_groups=mesh['row_0'=4,'row_1'=4,'col_0'=4,'col_1'=2] {'row_0','row_1'}, dimensions={0}, use_global_device_ids=true | all-gather | bytes 544 | tf_op jit(solution)/shard_map/all_gather | solution.py:46
  96.5 0.7 reduce.8
  97.1 0.1 reshape.383
  97.3 0.1 compare_and_fusion
  97.4 1.2 gather_fusion.4
  98.6 1.2 gather_fusion.5
  99.9 0.6 iota_compare_fusion.5
  100.4 0.1 fusion.37
  100.5 0.7 fusion.45
  101.2 5.0 %fusion.32 = pred[64]{0:T(512)(128)(4,1)S(1)} fusion(s32[]{:T(128)} %bitcast.20, s32[]{:T(128)} %bitcast.21, s32[]{:T(128)} %bitcast.22, s32[]{:T(128)} %bitcast.23, s32[]{:T(128)} %bitcast.24, s32[]{:T(128)} %bitcast.26, s32[]{:T(128)} %bitcast.25, s32[]{:T(128)} %bitcast.19), kind=kLoop, calls=%fused_computation.91 | loop fusion | flops 2880 | bytes 96 | tf_op jit(solution)/shard_map/lt | solution.py:82
  106.2 0.1 select_add_fusion
  106.3 0.1 add_and_fusion
  106.4 35.1 %all-gather.9.cloned.1.call-done = bf16[16,8,256,256]{3,2,1,0:T(8,128)(2,1)} async-done(((bf16[1,8,256,256]{3,2,1,0:T(8,128)(2,1)}), bf16[16,8,256,256]{3,2,1,0:T(8,128)(2,1)}) %all-gather.9.cloned.1.call-update) | async-done | bytes 16777232 | tf_op jit(solution)/shard_map/all_gather | solution.py:44
  141.5 11.8 %gather_fusion.3 = bf16[72,256,256]{2,1,0:T(8,128)(2,1)} fusion(bf16[128,256,256]{2,1,0:T(8,128)(2,1)} %bitcast.96, s32[1024]{0:T(1024)S(1)} %pad_clamp_fusion), kind=kCustom, calls=%fused_computation.5 | custom fusion | bytes 18874656 | tf_op jit(solution)/shard_map/jit(_take)/gather | solution.py:89
  153.3 13.3 %all-gather.11.cloned.1.call-done = bf16[2048,256]{1,0:T(8,128)(2,1)} async-done(((bf16[256,256]{1,0:T(8,128)(2,1)}), bf16[2048,256]{1,0:T(8,128)(2,1)}) %all-gather.11.cloned.1.call-update) | async-done | bytes 1048592 | tf_op jit(solution)/shard_map/all_gather | solution.py:26
  166.6 51.8 %all-gather.7.cloned.1.call-done = bf16[1,64,256,256]{3,2,0,1:T(8,128)(2,1)} async-done(((bf16[1,8,256,256]{3,2,0,1:T(8,128)(2,1)}), bf16[1,64,256,256]{3,2,0,1:T(8,128)(2,1)}) %all-gather.7.cloned.1.call-update) | async-done | bytes 8388624 | tf_op jit(solution)/shard_map/all_gather | solution.py:51
  218.4 13.5 %fusion.2 = f32[72,256,256]{2,1,0:T(8,128)} fusion(bf16[8,256,256]{2,1,0:T(8,128)(2,1)} %bitcast.105, bf16[64,256,256]{2,1,0:T(8,128)(2,1)} %bitcast.104, bf16[72,256,256]{2,1,0:T(8,128)(2,1)} %gather_fusion.3, pred[72]{0:T(512)(128)(4,1)S(1)} %get-tuple-element.16), kind=kOutput, calls=%fused_computation.8 | convolution fusion | flops 2425356288 | bytes 37748808 | tf_op jit(solution)/shard_map/axy,ayz->axz/dot_general | solution.py:94
  231.9 0.0 copy-start.1
  231.9 24.1 %fusion = f32[32,256,256]{2,0,1:T(8,128)S(1)} fusion(f32[72,256,256]{2,1,0:T(8,128)} %fusion.2, s32[72]{0:T(128)S(1)} %select_add_fusion, pred[72]{0:T(512)(128)(4,1)S(1)} %add_and_fusion), kind=kOutput, calls=%fused_computation.6 | convolution fusion | flops 1811943936 | bytes 27263336 | tf_op jit(solution)/shard_map/ap,axz->pxz/dot_general | solution.py:96
  256.0 0.0 copy-done.1
  256.0 5.2 %subtract_reduce_fusion = (f32[]{:T(128)}, bf16[32,256,256]{2,0,1:T(8,128)(2,1)}) fusion(f32[32,256,256]{2,0,1:T(8,128)S(1)} %fusion, bf16[16,256,256]{2,1,0:T(8,128)(2,1)S(1)} %bitcast.95, s32[16]{0:T(128)S(1)} %bitcast.101, pred[16]{0:T(512)(128)(4,1)S(1)} %iota_compare_fusion.6), kind=kOutput, calls=%fused_computation.14 | convolution fusion | flops 77595648 | bytes 14680148 | tf_op jit(solution)/shard_map/sp,sxz->pxz/dot_general | solution.py:99
  261.2 9.0 %psum.28 = f32[]{:T(128)} all-reduce(f32[]{:T(128)} %get-tuple-element.18), channel_id=1, replica_groups=mesh['row_0'=4,'row_1'=4,'col_0'=4,'col_1'=2] {'row_0'}, use_global_device_ids=true, to_apply=%region_5.7 | all-reduce | flops 1 | bytes 8 | tf_op jit(solution)/shard_map/psum | solution.py:32
  270.3 9.0 %psum.29 = f32[]{:T(128)} all-reduce(f32[]{:T(128)} %psum.28), channel_id=1, replica_groups=mesh['row_0'=4,'row_1'=4,'col_0'=4,'col_1'=2] {'row_1'}, use_global_device_ids=true, to_apply=%region_6.8 | all-reduce | flops 1 | bytes 8 | tf_op jit(solution)/shard_map/psum | solution.py:32
  279.3 7.1 %psum.30 = f32[]{:T(128)} all-reduce(f32[]{:T(128)} %psum.29), channel_id=1, replica_groups=mesh['row_0'=4,'row_1'=4,'col_0'=4,'col_1'=2] {'col_0'}, use_global_device_ids=true, to_apply=%region_7.9 | all-reduce | flops 1 | bytes 8 | tf_op jit(solution)/shard_map/psum | solution.py:32
  286.4 9.3 %psum.31 = f32[]{:T(128)} all-reduce(f32[]{:T(128)} %psum.30), channel_id=1, replica_groups=mesh['row_0'=4,'row_1'=4,'col_0'=4,'col_1'=2] {'col_1'}, use_global_device_ids=true, to_apply=%region_8.10 | all-reduce | flops 1 | bytes 8 | tf_op jit(solution)/shard_map/psum | solution.py:32
  295.6 2.5 copy.26
  298.1 4.2 %copy.28 = bf16[64,8,16,256]{3,1,2,0:T(8,128)(2,1)} copy(bf16[64,8,16,256]{3,2,1,0:T(8,128)(2,1)S(1)} %bitcast.93) | data formatting | bytes 8388608
  (19 shorter events, 0.1 us)
Async XLA Ops:
  8.0 49.4 %copy-start = (bf16[1,16,256,256]{3,2,1,0:T(8,128)(2,1)S(1)}, bf16[1,16,256,256]{3,2,1,0:T(8,128)(2,1)}, u32[]{:S(2)}) copy-start(bf16[1,16,256,256]{3,2,1,0:T(8,128)(2,1)} %param.8) | copy-start | bytes 6291460
  8.0 52.7 %copy-start.2 = (s32[1,8]{1,0:T(1,128)S(1)}, s32[1,8]{1,0:T(1,128)}, u32[]{:S(2)}) copy-start(s32[1,8]{1,0:T(1,128)} %param.12) | copy-start | bytes 100
  8.0 71.2 %copy-start.3 = (s32[1,8]{1,0:T(1,128)S(1)}, s32[1,8]{1,0:T(1,128)}, u32[]{:S(2)}) copy-start(s32[1,8]{1,0:T(1,128)} %param.13) | copy-start | bytes 100
  8.0 49.3 %reduce-scatter.2.cloned.1.call-start = ((), (), s32[]{:S(2)}) async-start(), calls=%async_computation.2 | async-start | bytes 1179648 | tf_op jit(solution)/shard_map/reduce_scatter | solution.py:23
  27.3 114.2 %all-gather.9.cloned.1.call-start = ((), (), s32[]{:S(2)}) async-start(), calls=%async_computation.3 | async-start | bytes 17825792 | tf_op jit(solution)/shard_map/all_gather | solution.py:44
  27.8 138.7 %all-gather.11.cloned.1.call-start = ((), (), s32[]{:S(2)}) async-start(), calls=%async_computation.4 | async-start | bytes 1179648 | tf_op jit(solution)/shard_map/all_gather | solution.py:26
  57.3 161.1 %all-gather.7.cloned.1.call-start = ((), (), s32[]{:S(2)}) async-start(), calls=%async_computation.1 | async-start | bytes 9437184 | tf_op jit(solution)/shard_map/all_gather | solution.py:51
  231.9 24.1 %copy-start.1 = (s32[1,16]{1,0:T(1,128)S(1)}, s32[1,16]{1,0:T(1,128)}, u32[]{:S(2)}) copy-start(s32[1,16]{1,0:T(1,128)} %param.9) | copy-start | bytes 196
Sparse Core Ops, SparseCore 0:
  27.4 29.8 reduce-scatter.1
Sparse Core Ops, SparseCore 1:
  29.9 111.5 all-gather.8
  143.1 23.5 all-gather.10
  168.8 49.6 all-gather.6
where the time goes:
time: 312 us
  waiting for transfers between devices  130 us (42%)
  blocking collectives  78.7 us (25%)
  matrix products  43.4 us (14%)
  local copies, waits for them, and re-layouts  31.2 us (10%)
  between operations  19.8 us (6%)
  other arithmetic  8.28 us (3%)
    all_gather x1, waiting for transfers between devices, on_device(): lax.all_gather(band_tiles[:, :half], COL, axis=1, tiled=True)  51.8 us
    all_gather x1, waiting for transfers between devices, on_device(): lax.all_gather(matrix_tiles, ROW, axis=0, tiled=True)  35.1 us
    psum x4, blocking collectives, over_axes(): shard = lax.psum(shard, axis)  34.4 us
    reduce_scatter x1, waiting for transfers between devices, sum_by_parts(): lax.psum_scatter(rows_for(lines, lax.axis_size(axis)), axis, scatter_dime...  29.4 us
    dot_general x1, matrix products, on_device(): jnp.einsum('ap,axz->pxz', weights, product, precision=lax.Precision.HIGHEST)  24.1 us
    all_gather x1, blocking collectives, on_device(): lax.all_gather(matrix_live, ROW, axis=0, tiled=True)  17.3 us
    all_gather x1, blocking collectives, on_device(): lax.all_gather(matrix_col, ROW, axis=0, tiled=True)  17.2 us
    dot_general x1, matrix products, on_device(): jnp.einsum('axy,ayz->axz', tiles, picked, preferred_element_type=jnp.floa...  13.5 us
  transfers between devices with their start and end apart: 4, of which 4 were waited for; matrix products, arithmetic and copies ran while one was open for 8% of the time, Pallas kernels for 0%

commit v1 on v0

--- a/solution.py
+++ b/solution.py
@@ -3,6 +3,7 @@
 from jax import lax
 from jax.sharding import Mesh
 from jax.sharding import PartitionSpec as P
+from jax.lax import all_to_all, axis_size
 
 TILES = 128
 BR = 2
@@ -41,7 +42,15 @@
     places = BR * tcols
     spots = jnp.arange(places, dtype=jnp.int32)
     b_tiles, b_index, b_live = (
-        lax.all_gather(matrix_tiles, ROW, axis=0, tiled=True),
+        jnp.concatenate(
+            all_to_all(
+                jnp.stack([matrix_tiles for _ in range(axis_size(ROW))]),
+                ROW,
+                concat_axis=0,
+                split_axis=0,
+            ),
+            axis=0,
+        ),
         lax.all_gather(matrix_col, ROW, axis=0, tiled=True),
         lax.all_gather(matrix_live, ROW, axis=0, tiled=True),
     )

time: 312 us -> 474 us (1.52)
  blocking collectives: 78.7 us -> 324 us
  waiting for transfers between devices: 130 us -> 29.7 us
  local copies, waits for them, and re-layouts: 31.2 us -> 42.1 us
  starting transfers between devices: 0.16 us -> 6.96 us
    all_gather x1, blocking collectives: 17.2 us -> 247 us  [on_device(): lax.all_gather(matrix_col, ROW, axis=0, tiled=True)]
    all_gather x1, waiting for transfers between devices: 51.8 us -> 0.01 us  [on_device(): lax.all_gather(band_tiles[:, :half], COL, axis=1, tiled=True)]
    all_gather x1 -> x0, waiting for transfers between devices: 35.1 us -> none  [on_device(): lax.all_gather(matrix_tiles, ROW, axis=0, tiled=True)]
    psum x4, blocking collectives: 34.4 us -> 54.5 us  [over_axes(): shard = lax.psum(shard, axis)]
    all_gather x1, waiting for transfers between devices: 13.3 us -> 0.01 us  [sum_by_parts(): whole = lax.all_gather(own, axis).reshape(-1, *lines.shape[1:])]
    all_to_all x0 -> x1, starting transfers between devices: none -> 6.84 us  [on_device(): all_to_all(jnp.stack([matrix_tiles for _ in range(axis_size(ROW))]), ROW,...]
    another operation x0 -> x1, local copies, waits for them, and re-layouts: none -> 6.81 us  [on_device(): jnp.stack([matrix_tiles for _ in range(axis_size(ROW))])]
  transfers between devices with their start and end apart: 4 -> 4, of which waited for: 4 -> 1; matrix products, arithmetic and copies ran while one was open for 8% -> 7% of each run, Pallas kernels for 0% -> 0%
where the time goes in v1:
time: 474 us; the launch traced here: 473 us
  blocking collectives  324 us (68%)
  matrix products  43.5 us (9%)
  local copies, waits for them, and re-layouts  42.1 us (9%)
  waiting for transfers between devices  29.7 us (6%)
  between operations  17.7 us (4%)
  other arithmetic  8.48 us (2%)
  starting transfers between devices  6.96 us (1%)
    all_gather x1, blocking collectives, on_device(): lax.all_gather(matrix_col, ROW, axis=0, tiled=True)  247 us
    psum x4, blocking collectives, over_axes(): shard = lax.psum(shard, axis)  54.5 us
    reduce_scatter x1, waiting for transfers between devices, sum_by_parts(): lax.psum_scatter(rows_for(lines, lax.axis_size(axis)), axis, scatter_dime...  29.7 us
    dot_general x1, matrix products, on_device(): jnp.einsum('ap,axz->pxz', weights, product, precision=lax.Precision.HIGHEST)  24.1 us
    all_gather x1, blocking collectives, on_device(): lax.all_gather(matrix_live, ROW, axis=0, tiled=True)  13.6 us
    dot_general x1, matrix products, on_device(): jnp.einsum('axy,ayz->axz', tiles, picked, preferred_element_type=jnp.floa...  13.5 us
    gather x1, local copies, waits for them, and re-layouts, on_device(): picked = jnp.take(flat_tiles, k_glob, axis=0)  11.8 us
    unnamed x1, blocking collectives  9.78 us
  transfers between devices with their start and end apart: 4, of which 1 were waited for; matrix products, arithmetic and copies ran while one was open for 7% of the time, Pallas kernels for 0%

profile of v1, /device:TPU:1, one launch (start us, length us, event | category | flops | bytes accessed | tf_op | source)
XLA Modules:
  0.0 472.9 jit_solution(10398335396985986402)
XLA Ops:
  7.2 0.0 reduce-scatter.2.cloned.1.call-start
  7.9 1.2 dynamic-slice.3
  9.8 0.7 bitcast_dynamic-update-slice_fusion
  10.5 0.8 bitcast_dynamic-update-slice_fusion.1
  11.2 9.8 %all-reduce.2 = (s32[8]{0:T(128)S(1)}, s32[128]{0:T(128)S(1)}) all-reduce(s32[8]{0:T(128)S(1)} %bitcast_dynamic-update-slice_fusion, s32[128]{0:T(128)S(1)} %bitcast_dynamic-update-slice_fusion.1), channel_id=1, replica_groups=mesh['row_0'=4,'row_1'=4,'col_0'=4,'col_1'=2] {'col_0','col_1'}, use_global_device_ids=true, to_apply=%add.1 | all-reduce | flops 136 | bytes 1088
  21.0 0.7 fusion.42
  21.7 0.2 reduce-window.8
  21.9 0.6 dynamic-slice.2
  23.1 1.3 slice.7
  24.4 0.7 convolution_convert_fusion
  25.1 1.2 copy.24
  26.3 0.0 reduce-scatter.2.cloned.1.call-update
  26.3 0.0 all-gather.8.cloned.1.call-start
  26.4 29.7 %reduce-scatter.2.cloned.1.call-done = bf16[256,256]{1,0:T(8,128)(2,1)} async-done(((bf16[2048,256]{1,0:T(8,128)(2,1)}), bf16[256,256]{1,0:T(8,128)(2,1)}) %reduce-scatter.2.cloned.1.call-update) | async-done | bytes 131088 | tf_op jit(solution)/shard_map/reduce_scatter | solution.py:24
  56.1 0.0 all-gather.8.cloned.1.call-update
  56.1 6.8 %stack.2 = bf16[16,1,8,256,256]{4,3,2,1,0:T(8,128)(2,1)} broadcast(bf16[8,256,256]{2,1,0:T(8,128)(2,1)} %bitcast.99), dimensions={2,3,4} | broadcast | bytes 17825792 | tf_op jit(solution)/shard_map/stack | solution.py:47
  62.9 0.0 copy-start
  62.9 0.0 copy-start.2
  62.9 0.0 copy-start.3
  62.9 6.8 %all-to-all-start = ((bf16[16,1,8,256,256]{4,3,2,1,0:T(8,128)(2,1)}), bf16[16,1,8,256,256]{4,3,2,1,0:T(8,128)(2,1)}, u32[]{:S(2)}, u32[]{:S(2)}) async-start(bf16[16,1,8,256,256]{4,3,2,1,0:T(8,128)(2,1)} %stack.2), calls=%async_computation.1 | async-start | bytes 33554432 | tf_op jit(solution)/shard_map/all_to_all | solution.py:46
  69.8 0.0 all-gather.6.cloned.1.call-start
  69.8 0.0 copy-done
  69.8 1.0 slice.43
  70.9 0.0 all-gather.6.cloned.1.call-update
  70.9 0.1 convert_reduce_fusion
  71.0 0.6 gather_fusion.1
  71.7 0.6 gather_fusion.2
  72.4 0.8 gather_fusion
  73.2 0.0 copy-done.2
  73.2 246.5 %all-gather.1 = s32[16,1,8]{2,1,0:T(1,128)S(1)} all-gather(s32[1,1,8]{2,1,0:T(1,128)S(1)} %bitcast.103), channel_id=1, replica_groups=mesh['row_0'=4,'row_1'=4,'col_0'=4,'col_1'=2] {'row_0','row_1'}, dimensions={0}, use_global_device_ids=true | all-gather | bytes 544 | tf_op jit(solution)/shard_map/all_gather | solution.py:54
  319.7 0.5 broadcast.1068
  320.2 0.7 reduce.7
  320.8 0.1 reshape.382
  320.9 0.0 copy-done.3
  320.9 13.6 %all-gather.2 = s32[16,1,8]{2,1,0:T(1,128)S(1)} all-gather(s32[1,1,8]{2,1,0:T(1,128)S(1)} %bitcast.104), channel_id=1, replica_groups=mesh['row_0'=4,'row_1'=4,'col_0'=4,'col_1'=2] {'row_0','row_1'}, dimensions={0}, use_global_device_ids=true | all-gather | bytes 544 | tf_op jit(solution)/shard_map/all_gather | solution.py:55
  334.5 0.7 reduce.8
  335.2 0.1 reshape.383
  335.3 0.1 compare_and_fusion
  335.4 1.2 gather_fusion.4
  336.6 1.2 gather_fusion.5
  337.9 0.6 iota_compare_fusion.5
  338.6 0.1 fusion.37
  338.6 0.7 fusion.45
  339.3 5.1 %fusion.32 = pred[64]{0:T(512)(128)(4,1)S(1)} fusion(s32[]{:T(128)} %bitcast.20, s32[]{:T(128)} %bitcast.21, s32[]{:T(128)} %bitcast.22, s32[]{:T(128)} %bitcast.23, s32[]{:T(128)} %bitcast.24, s32[]{:T(128)} %bitcast.26, s32[]{:T(128)} %bitcast.25, s32[]{:T(128)} %bitcast.19), kind=kLoop, calls=%fused_computation.91 | loop fusion | flops 2880 | bytes 96 | tf_op jit(solution)/shard_map/lt | solution.py:91
  344.4 0.1 select_add_fusion
  344.5 0.1 add_and_fusion
  344.6 0.0 all-to-all-done
  344.6 11.8 %gather_fusion.3 = bf16[72,256,256]{2,1,0:T(8,128)(2,1)} fusion(bf16[128,256,256]{2,1,0:T(8,128)(2,1)} %bitcast.38, s32[1024]{0:T(1024)S(1)} %pad_clamp_fusion), kind=kCustom, calls=%fused_computation.5 | custom fusion | bytes 18874656 | tf_op jit(solution)/shard_map/jit(_take)/gather | solution.py:98
  356.4 0.0 all-gather.8.cloned.1.call-done
  356.4 0.0 all-gather.6.cloned.1.call-done
  356.4 13.5 %fusion.2 = f32[72,256,256]{2,1,0:T(8,128)} fusion(bf16[8,256,256]{2,1,0:T(8,128)(2,1)} %bitcast.106, bf16[64,256,256]{2,1,0:T(8,128)(2,1)} %bitcast.105, bf16[72,256,256]{2,1,0:T(8,128)(2,1)} %gather_fusion.3, pred[72]{0:T(512)(128)(4,1)S(1)} %get-tuple-element.16), kind=kOutput, calls=%fused_computation.8 | convolution fusion | flops 2425356288 | bytes 37748808 | tf_op jit(solution)/shard_map/axy,ayz->axz/dot_general | solution.py:103
  369.9 0.0 copy-start.1
  369.9 24.1 %fusion = f32[32,256,256]{2,0,1:T(8,128)S(1)} fusion(f32[72,256,256]{2,1,0:T(8,128)} %fusion.2, s32[72]{0:T(128)S(1)} %select_add_fusion, pred[72]{0:T(512)(128)(4,1)S(1)} %add_and_fusion), kind=kOutput, calls=%fused_computation.6 | convolution fusion | flops 1811943936 | bytes 27263336 | tf_op jit(solution)/shard_map/ap,axz->pxz/dot_general | solution.py:105
  394.0 0.0 copy-done.1
  394.0 5.2 %subtract_reduce_fusion = (f32[]{:T(128)}, bf16[32,256,256]{2,0,1:T(8,128)(2,1)}) fusion(f32[32,256,256]{2,0,1:T(8,128)S(1)} %fusion, bf16[16,256,256]{2,1,0:T(8,128)(2,1)S(1)} %bitcast.96, s32[16]{0:T(128)S(1)} %bitcast.102, pred[16]{0:T(512)(128)(4,1)S(1)} %iota_compare_fusion.6), kind=kOutput, calls=%fused_computation.14 | convolution fusion | flops 77595648 | bytes 14680148 | tf_op jit(solution)/shard_map/sp,sxz->pxz/dot_general | solution.py:108
  399.2 8.0 %psum.28 = f32[]{:T(128)} all-reduce(f32[]{:T(128)} %get-tuple-element.18), channel_id=1, replica_groups=mesh['row_0'=4,'row_1'=4,'col_0'=4,'col_1'=2] {'row_0'}, use_global_device_ids=true, to_apply=%region_5.7 | all-reduce | flops 1 | bytes 8 | tf_op jit(solution)/shard_map/psum | solution.py:33
  407.3 6.9 %psum.29 = f32[]{:T(128)} all-reduce(f32[]{:T(128)} %psum.28), channel_id=1, replica_groups=mesh['row_0'=4,'row_1'=4,'col_0'=4,'col_1'=2] {'row_1'}, use_global_device_ids=true, to_apply=%region_6.8 | all-reduce | flops 1 | bytes 8 | tf_op jit(solution)/shard_map/psum | solution.py:33
  414.2 4.4 copy.26
  418.6 22.1 %psum.30 = f32[]{:T(128)} all-reduce(f32[]{:T(128)} %psum.29), channel_id=1, replica_groups=mesh['row_0'=4,'row_1'=4,'col_0'=4,'col_1'=2] {'col_0'}, use_global_device_ids=true, to_apply=%region_7.9 | all-reduce | flops 1 | bytes 8 | tf_op jit(solution)/shard_map/psum | solution.py:33
  440.7 6.4 %copy.28 = bf16[64,8,16,256]{3,1,2,0:T(8,128)(2,1)} copy(bf16[64,8,16,256]{3,2,1,0:T(8,128)(2,1)} %bitcast.94) | data formatting | bytes 8388608
  447.1 17.5 %psum.31 = f32[]{:T(128)} all-reduce(f32[]{:T(128)} %psum.30), channel_id=1, replica_groups=mesh['row_0'=4,'row_1'=4,'col_0'=4,'col_1'=2] {'col_1'}, use_global_device_ids=true, to_apply=%region_8.10 | all-reduce | flops 1 | bytes 8 | tf_op jit(solution)/shard_map/psum | solution.py:33
  (19 shorter events, 0.1 us)
Async XLA Ops:
  7.2 48.9 %reduce-scatter.2.cloned.1.call-start = ((), (), s32[]{:S(2)}) async-start(), calls=%async_computation.3 | async-start | bytes 1179648 | tf_op jit(solution)/shard_map/reduce_scatter | solution.py:24
  26.3 330.0 %all-gather.8.cloned.1.call-start = ((), (), s32[]{:S(2)}) async-start(), calls=%async_computation.4 | async-start | bytes 1179648 | tf_op jit(solution)/shard_map/all_gather | solution.py:27
  62.9 6.9 %copy-start = (bf16[1,16,256,256]{3,2,1,0:T(8,128)(2,1)S(1)}, bf16[1,16,256,256]{3,2,1,0:T(8,128)(2,1)}, u32[]{:S(2)}) copy-start(bf16[1,16,256,256]{3,2,1,0:T(8,128)(2,1)} %param.8) | copy-start | bytes 6291460
  62.9 10.3 %copy-start.2 = (s32[1,8]{1,0:T(1,128)S(1)}, s32[1,8]{1,0:T(1,128)}, u32[]{:S(2)}) copy-start(s32[1,8]{1,0:T(1,128)} %param.12) | copy-start | bytes 100
  62.9 258.0 %copy-start.3 = (s32[1,8]{1,0:T(1,128)S(1)}, s32[1,8]{1,0:T(1,128)}, u32[]{:S(2)}) copy-start(s32[1,8]{1,0:T(1,128)} %param.13) | copy-start | bytes 100
  62.9 281.6 %all-to-all-start = ((bf16[16,1,8,256,256]{4,3,2,1,0:T(8,128)(2,1)}), bf16[16,1,8,256,256]{4,3,2,1,0:T(8,128)(2,1)}, u32[]{:S(2)}, u32[]{:S(2)}) async-start(bf16[16,1,8,256,256]{4,3,2,1,0:T(8,128)(2,1)} %stack.2), calls=%async_computation.1 | async-start | bytes 33554432 | tf_op jit(solution)/shard_map/all_to_all | solution.py:46
  69.8 286.6 %all-gather.6.cloned.1.call-start = ((), (), s32[]{:S(2)}) async-start(), calls=%async_computation.2 | async-start | bytes 9437184 | tf_op jit(solution)/shard_map/all_gather | solution.py:60
  369.9 24.1 %copy-start.1 = (s32[1,16]{1,0:T(1,128)S(1)}, s32[1,16]{1,0:T(1,128)}, u32[]{:S(2)}) copy-start(s32[1,16]{1,0:T(1,128)} %param.9) | copy-start | bytes 196
Sparse Core Ops, SparseCore 0:
  26.5 29.5 reduce-scatter.1
  57.8 25.6 all-gather.7
  85.8 49.8 all-gather.5
